TPU v7x, 128 devices: a whole 4x4x4 slice. The times are simulated.
128 devices in a mesh: ctx: 32 (over z, y, core), tp: 4 (over x).
Axes of the slice: x: 4, y: 4, z: 4, core: 2. Of those that a mesh axis runs over, the one named last changes fastest.
Arguments:
- x_tokens: bfloat16 [16384, 4096], P('ctx', 'tp'), may hold values from -60 to 60
- w_query: bfloat16 [4096, 4096], P(None, 'tp'), may hold values from -0.09375 to 0.09375
- w_key: bfloat16 [4096, 1024], P(None, 'tp'), may hold values from -0.09375 to 0.09375
- w_value: bfloat16 [4096, 1024], P(None, 'tp'), may hold values from -0.09375 to 0.09375
- w_output: bfloat16 [4096, 4096], P('tp'), may hold values from -0.09375 to 0.09375
- pattern: int32 [128, 8], P('ctx'), may hold values from 0 to 127, as said below
- doc_lengths: int32 [16], replicated, may hold values from 1 to 10240, 16384 in all
Outputs:
- attn_out: bfloat16 [16384, 4096], P(('ctx', 'tp'))
Inputs may be any that keep to these rules, and one draw needn't show every extreme that they name: `pattern`: row q has 8 entries; the first is q itself and every entry is at most q; entries may repeat. The rows of one index of ctx (4 rows) name at most 2 distinct blocks held by any other index of ctx (index i holding blocks i * 4 onward), and exactly 2 of index 0 for every other index. Every row of an index i in the upper half of ctx names 2 blocks of index i minus half the number of ctx indices.
All inputs are finite; a program needn't handle non-finite values.
Results may differ from a plain program's by a relative error of at most 0.02.
Values may be sent and summed in bfloat16 or wider, within the bound.
No kernel may reach another device: no remote copies, remote signals or barrier semaphores. Data moves between devices by JAX's collectives and lax.ppermute only.
A program may use at most 128 MiB of HBM per device.

v0:
```python
import jax
import jax.numpy as jnp
from jax import lax
from jax.sharding import PartitionSpec as P

HD = 128
BLK = 128
LIST = 8
ROPE_BASE = 500000.0
NEG_LARGE = -1e30


def rotate(projected, head_count, positions):
    split_heads = projected.reshape(projected.shape[0], head_count, HD)
    frequency = ROPE_BASE ** (-(jnp.arange(HD // 2, dtype=jnp.float32) * 2.0 / HD))
    angles = positions.astype(jnp.float32)[:, None] * frequency[None, :]
    cosine_table = jnp.cos(angles)[:, None, :]
    sine_table = jnp.sin(angles)[:, None, :]
    front_half = split_heads[..., : HD // 2]
    back_half = split_heads[..., HD // 2 :]
    return jnp.concatenate(
        [
            front_half * cosine_table - back_half * sine_table,
            back_half * cosine_table + front_half * sine_table,
        ],
        axis=-1,
    )


def document_of(positions, doc_lengths):
    ends = jnp.cumsum(doc_lengths)
    return jnp.sum((ends[None, :] <= positions[:, None]).astype(jnp.int32), axis=1)


def fresh_entries(pattern):
    equal = pattern[:, :, None] == pattern[:, None, :]
    earlier = jnp.tril(jnp.ones((LIST, LIST), dtype=bool), -1)
    return jnp.logical_not(jnp.any(equal & earlier[None], axis=2))


def attend_listed(
    query,
    chosen_keys,
    chosen_values,
    pattern,
    positions,
    documents,
    doc_lengths,
    kv_heads,
    group_size,
):
    local_rows = positions.shape[0]
    block_count = local_rows // BLK
    fresh = fresh_entries(pattern)
    offsets_in = jnp.arange(BLK, dtype=jnp.int32)
    key_index = (pattern[:, :, None] * BLK + offsets_in[None, None, :]).reshape(
        block_count, LIST * BLK
    )
    key_ok = jnp.repeat(fresh, BLK, axis=1)
    key_doc = document_of(key_index.reshape(-1), doc_lengths).reshape(key_index.shape)
    block_pos = positions.reshape(block_count, BLK)
    block_doc = documents.reshape(block_count, BLK)
    block_query = query.reshape(block_count, BLK, kv_heads, group_size, HD)
    allowed = (
        (key_index[:, None, :] <= block_pos[:, :, None])
        & (key_doc[:, None, :] == block_doc[:, :, None])
        & key_ok[:, None, :]
    )
    allowed = allowed[:, None, None, :, :]
    scores = jnp.einsum(
        "bqkgd,blkd->bkgql", block_query, chosen_keys, preferred_element_type=jnp.float32
    )
    masked = jnp.where(allowed, scores, NEG_LARGE)
    row_max = jnp.max(masked, axis=-1, keepdims=True)
    weights = jnp.where(allowed, jnp.exp(masked - row_max), 0.0)
    total = jnp.sum(weights, axis=-1)
    mixed = jnp.einsum(
        "bkgql,blkd->bkgqd",
        weights.astype(jnp.bfloat16),
        chosen_values,
        preferred_element_type=jnp.float32,
    )
    mixed = mixed / total[..., None]
    return (
        jnp.transpose(mixed, (0, 3, 1, 2, 4))
        .reshape(local_rows, kv_heads * group_size * HD)
        .astype(jnp.bfloat16)
    )


def on_device(x_tokens, w_query, w_key, w_value, w_output, pattern, doc_lengths):
    features = lax.all_gather(x_tokens, "tp", axis=1, tiled=True)
    local_rows = features.shape[0]
    query_heads = w_query.shape[1] // HD
    kv_heads = w_key.shape[1] // HD
    group_size = query_heads // kv_heads
    block_count = local_rows // BLK
    positions = lax.axis_index("ctx") * local_rows + jnp.arange(local_rows, dtype=jnp.int32)
    query = rotate(
        jnp.dot(features, w_query, preferred_element_type=jnp.float32), query_heads, positions
    ) * HD ** (-0.5)
    query = query.astype(jnp.bfloat16).reshape(local_rows, kv_heads, group_size, HD)
    keys = rotate(jnp.dot(features, w_key, preferred_element_type=jnp.float32), kv_heads, positions)
    keys = keys.astype(jnp.bfloat16).reshape(local_rows, kv_heads * HD)
    values = jnp.dot(features, w_value, preferred_element_type=jnp.float32).astype(jnp.bfloat16)
    documents = document_of(positions, doc_lengths)
    every_key, every_value = (
        lax.all_gather(keys, "ctx", axis=0, tiled=True),
        lax.all_gather(values, "ctx", axis=0, tiled=True),
    )
    offsets_in = jnp.arange(BLK, dtype=jnp.int32)
    key_index = (pattern[:, :, None] * BLK + offsets_in[None, None, :]).reshape(
        block_count, LIST * BLK
    )
    chosen_keys = every_key[key_index].reshape(block_count, LIST * BLK, kv_heads, HD)
    chosen_values = every_value[key_index].reshape(block_count, LIST * BLK, kv_heads, HD)
    attended = attend_listed(
        query,
        chosen_keys,
        chosen_values,
        pattern,
        positions,
        documents,
        doc_lengths,
        kv_heads,
        group_size,
    )
    return lax.psum_scatter(
        jnp.dot(attended, w_output, preferred_element_type=jnp.float32).astype(jnp.bfloat16),
        "tp",
        scatter_dimension=0,
        tiled=True,
    )


def solution(mesh):
    return jax.shard_map(
        on_device,
        mesh=mesh,
        in_specs=(
            P("ctx", "tp"),
            P(None, "tp"),
            P(None, "tp"),
            P(None, "tp"),
            P("tp", None),
            P("ctx", None),
            P(),
        ),
        out_specs=P(("ctx", "tp"), None),
        check_vma=False,
    )
```

profile of v0, /device:TPU:1, one launch (start us, length us, event | category | flops | bytes accessed | tf_op | source)
XLA Modules:
  0.0 297.7 jit_solution(13942825732113829720)
XLA Ops:
  6.5 0.0 copy-start
  6.5 0.0 all-gather.4.cloned.1.call-start
  6.5 0.7 all-gather.4.cloned.1.call-update
  7.3 0.0 all-gather.8.cloned.1.call-start
  7.3 53.2 %all-gather.4.cloned.1.call-done = bf16[512,4096]{1,0:T(8,128)(2,1)} async-done(((bf16[512,1024]{1,0:T(8,128)(2,1)}), bf16[512,4096]{1,0:T(8,128)(2,1)}) %all-gather.4.cloned.1.call-update) | async-done | bytes 4194320 | tf_op jit(solution)/shard_map/all_gather | solution.py:92
  60.5 0.0 copy-done
  60.5 4.1 %convolution_convert_fusion.1 = bf16[512,256]{1,0:T(8,128)(2,1)} fusion(bf16[512,4096]{1,0:T(8,128)(2,1)} %all-gather.4.cloned.1.call-done, bf16[4096,256]{1,0:T(8,128)(2,1)S(1)} %copy-done), kind=kOutput, calls=%fused_computation.19 | convolution fusion | flops 1073872896 | bytes 6553600 | tf_op jit(solution)/shard_map/dot_general | solution.py:105
  64.6 0.0 all-gather.8.cloned.1.call-update
  64.6 0.0 all-gather.6.cloned.1.call-start
  64.7 0.5 multiply_cosine_fusion
  65.2 4.2 %fusion.23 = f32[512,256]{0,1:T(8,128)S(1)} fusion(bf16[512,4096]{1,0:T(8,128)(2,1)} %all-gather.4.cloned.1.call-done, bf16[4096,256]{1,0:T(8,128)(2,1)} %param.9), kind=kOutput, calls=%fused_computation.51 | convolution fusion | flops 1073741824 | bytes 6815744 | tf_op jit(solution)/shard_map/dot_general | solution.py:103
  69.4 0.0 copy-start.4
  69.4 0.0 copy-start.5
  69.4 0.1 subtract_convert_fusion
  69.6 0.9 copy.38
  70.4 0.0 all-gather.6.cloned.1.call-update
  70.4 0.2 reduce-scatter.2.cloned.1.call-start
  70.7 0.1 iota_compare_fusion
  70.8 0.0 copy-done.4
  70.8 0.2 and_reduce_fusion
  71.0 0.1 broadcast_bitcast_fusion.1
  71.1 0.1 copy.25
  71.2 0.1 reduce
  71.3 0.1 add.112
  71.4 0.1 broadcast_bitcast_fusion
  71.5 0.1 convert_reduce_fusion
  71.7 0.1 convert_reduce_fusion.1
  71.8 3.9 %and_and_fusion = pred[4,128,1024]{1,2,0:T(8,128)(4,1)} fusion(s32[4,128]{1,0:T(4,128)S(1)} %bitcast.60, s32[4,1024]{1,0:T(4,128)S(1)} %eq.34, s32[4,128]{1,0:T(4,128)S(1)} %add_add_fusion, s32[4,1024]{1,0:T(4,128)S(1)} %bitcast_add_fusion, pred[4,1024]{1,0:T(4,128)(4,1)S(1)} %bitcast.59), kind=kLoop, calls=%fused_computation.18 | loop fusion | flops 2097152 | bytes 565248 | tf_op jit(solution)/shard_map/and | solution.py:65
  75.7 8.3 %fusion.24 = f32[512,1024]{0,1:T(8,128)S(1)} fusion(bf16[512,4096]{1,0:T(8,128)(2,1)} %all-gather.4.cloned.1.call-done, bf16[4096,1024]{1,0:T(8,128)(2,1)} %param.8), kind=kOutput, calls=%fused_computation.52 | convolution fusion | flops 4294967296 | bytes 14680064 | tf_op jit(solution)/shard_map/reshape | solution.py:14
  84.0 0.3 multiply_subtract_fusion
  84.3 1.3 concatenate.13
  85.6 1.7 copy.29
  87.4 1.3 concatenate.14
  88.7 2.7 copy.30
  91.4 27.2 %all-gather.8.cloned.1.call-done = bf16[16384,256]{1,0:T(8,128)(2,1)} async-done(((bf16[512,256]{1,0:T(8,128)(2,1)}), bf16[16384,256]{1,0:T(8,128)(2,1)}) %all-gather.8.cloned.1.call-update) | async-done | bytes 8388624 | tf_op jit(solution)/shard_map/all_gather | solution.py:109
  118.6 20.4 %gather_fusion.1 = bf16[4096,256]{1,0:T(8,128)(2,1)} fusion(bf16[16384,256]{1,0:T(8,128)(2,1)} %all-gather.8.cloned.1.call-done, s32[4096]{0:T(1024)S(1)} %bitcast_clamp_fusion), kind=kCustom, calls=%fused_computation.1 | custom fusion | bytes 4210688 | tf_op jit(solution)/shard_map/gather | solution.py:116
  139.0 4.0 %reshape.220 = bf16[4,1024,2,128]{3,2,1,0:T(2,128)(2,1)} reshape(bf16[4096,256]{1,0:T(8,128)(2,1)} %gather_fusion.1) | data formatting | bytes 4194304 | tf_op jit(solution)/shard_map/reshape | solution.py:116
  143.0 30.5 %all-gather.6.cloned.1.call-done = bf16[16384,256]{1,0:T(8,128)(2,1)} async-done(((bf16[512,256]{1,0:T(8,128)(2,1)}), bf16[16384,256]{1,0:T(8,128)(2,1)}) %all-gather.6.cloned.1.call-update) | async-done | bytes 8388624 | tf_op jit(solution)/shard_map/all_gather | solution.py:108
  173.4 20.4 %gather_fusion = bf16[4096,256]{1,0:T(8,128)(2,1)} fusion(bf16[16384,256]{1,0:T(8,128)(2,1)} %all-gather.6.cloned.1.call-done, s32[4096]{0:T(1024)S(1)} %bitcast_clamp_fusion), kind=kCustom, calls=%fused_computation | custom fusion | bytes 4210688 | tf_op jit(solution)/shard_map/gather | solution.py:115
  193.8 4.0 %reshape.218 = bf16[4,1024,2,128]{3,2,1,0:T(2,128)(2,1)} reshape(bf16[4096,256]{1,0:T(8,128)(2,1)} %gather_fusion) | data formatting | bytes 4194304 | tf_op jit(solution)/shard_map/reshape | solution.py:115
  197.8 10.5 %fusion.9 = f32[4,2,1024,128,4]{3,2,4,1,0:T(8,128)} fusion(bf16[4,1024,2,128,1]{3,2,1,0,4:T(2,128)(2,1)} %bitcast.54, f32[4,128,2,4,64]{4,1,3,2,0:T(8,128)} %copy.30, f32[4,128,2,4,64]{4,1,3,2,0:T(8,128)S(1)} %copy.29), kind=kOutput, calls=%fused_computation.16 | convolution fusion | flops 1075314688 | bytes 20971520 | tf_op jit(solution)/shard_map/bqkgd,blkd->bkgql/dot_general | solution.py:70
  208.3 19.6 %fusion.22 = (f32[4,2,4,128]{3,2,1,0:T(4,128)S(1)}, bf16[4,2,4,128,1024]{3,4,2,1,0:T(8,128)(2,1)}) fusion(f32[4,2,1024,128,4]{3,2,4,1,0:T(8,128)} %fusion.9, pred[4,128,1024]{1,2,0:T(8,128)(4,1)S(1)} %copy-done.3), kind=kOutput, calls=%fused_computation.50 | output fusion | flops 25166848 | bytes 25706496 | tf_op jit(solution)/shard_map/sub | solution.py:75
  227.9 6.2 %fusion.7 = bf16[4,128,2,4,128]{4,1,3,2,0:T(8,128)(2,1)S(1)} fusion(f32[4,128,2,4]{1,3,2,0:T(4,128)S(1)} %bitcast.62, bf16[4,1024,2,128,1]{3,2,1,0,4:T(2,128)(2,1)S(1)} %bitcast.55, bf16[4,2,4,128,1024]{3,4,2,1,0:T(8,128)(2,1)} %get-tuple-element.14), kind=kOutput, calls=%fused_computation.14 | convolution fusion | flops 1074790400 | bytes 11550720 | tf_op jit(solution)/shard_map/bkgql,blkd->bkgqd/dot_general | solution.py:77
  234.1 0.8 copy.34
  234.9 0.8 convert_element_type.46
  235.7 9.4 %convolution_convert_fusion = bf16[512,4096]{1,0:T(8,128)(2,1)} fusion(bf16[512,1024]{1,0:T(8,128)(2,1)S(1)} %convert_element_type.46, bf16[1024,4096]{1,0:T(8,128)(2,1)} %param.11), kind=kOutput, calls=%fused_computation.10 | convolution fusion | flops 4297064448 | bytes 13631488 | tf_op jit(solution)/shard_map/dot_general | solution.py:129
  245.1 0.0 reduce-scatter.2.cloned.1.call-update
  245.1 46.0 %reduce-scatter.2.cloned.1.call-done = bf16[128,4096]{1,0:T(8,128)(2,1)} async-done(((bf16[512,4096]{1,0:T(8,128)(2,1)}), bf16[128,4096]{1,0:T(8,128)(2,1)}) %reduce-scatter.2.cloned.1.call-update) | async-done | bytes 1048592 | tf_op jit(solution)/shard_map/reduce_scatter | solution.py:128
  (22 shorter events, 0.2 us)
Async XLA Ops:
  6.5 53.9 %copy-start = (bf16[4096,256]{1,0:T(8,128)(2,1)S(1)}, bf16[4096,256]{1,0:T(8,128)(2,1)}, u32[]{:S(2)}) copy-start(bf16[4096,256]{1,0:T(8,128)(2,1)} %param.10) | copy-start | bytes 6291460
  6.5 53.9 %all-gather.4.cloned.1.call-start = ((), (), s32[]{:S(2)}) async-start(), calls=%async_computation.1 | async-start | bytes 5242880 | tf_op jit(solution)/shard_map/all_gather | solution.py:92
  7.3 111.4 %all-gather.8.cloned.1.call-start = ((), (), s32[]{:S(2)}) async-start(), calls=%async_computation.3 | async-start | bytes 8650752 | tf_op jit(solution)/shard_map/all_gather | solution.py:109
  64.6 108.8 %all-gather.6.cloned.1.call-start = ((), (), s32[]{:S(2)}) async-start(), calls=%async_computation.2 | async-start | bytes 8650752 | tf_op jit(solution)/shard_map/all_gather | solution.py:108
  69.4 1.4 copy-start.4
  69.4 1.7 copy-start.5
  70.4 220.7 %reduce-scatter.2.cloned.1.call-start = ((), (), s32[]{:S(2)}) async-start(), calls=%async_computation.4 | async-start | bytes 5242880 | tf_op jit(solution)/shard_map/reduce_scatter | solution.py:128
  197.8 10.5 %copy-start.3 = (pred[4,128,1024]{1,2,0:T(8,128)(4,1)S(1)}, pred[4,128,1024]{1,2,0:T(8,128)(4,1)}, u32[]{:S(2)}) copy-start(pred[4,128,1024]{1,2,0:T(8,128)(4,1)} %and_and_fusion) | copy-start | bytes 1572868
  208.3 19.6 %copy-start.2 = (bf16[4,1024,2,128]{3,2,1,0:T(2,128)(2,1)S(1)}, bf16[4,1024,2,128]{3,2,1,0:T(2,128)(2,1)}, u32[]{:S(2)}) copy-start(bf16[4,1024,2,128]{3,2,1,0:T(2,128)(2,1)} %reshape.220) | copy-start | bytes 6291460
  245.1 46.1 %copy-start.1 = (bf16[4096,256]{1,0:T(8,128)(2,1)S(1)}, bf16[4096,256]{1,0:T(8,128)(2,1)}, u32[]{:S(2)}) copy-start(bf16[4096,256]{1,0:T(8,128)(2,1)} %param.10) | copy-start | bytes 6291460
Sparse Core Ops, SparseCore 0:
  9.0 51.3 all-gather.3
  64.7 53.8 all-gather.7
  120.9 52.5 all-gather.5
  245.2 45.8 reduce-scatter.1
where the time goes:
time: 298 us
  waiting for transfers between devices  158 us (53%)
  local copies, waits for them, and re-layouts  58.6 us (20%)
  matrix products  42.6 us (14%)
  other arithmetic  25.3 us (8%)
  between operations  13.3 us (4%)
    all_gather x1, waiting for transfers between devices, on_device(): features = lax.all_gather(x_tokens, 'tp', axis=1, tiled=True)  53.2 us
    reduce_scatter x1, waiting for transfers between devices, on_device(): lax.psum_scatter(jnp.dot(attended, w_output, preferred_element_type=jnp.f...  46 us
    all_gather x1, waiting for transfers between devices, on_device(): lax.all_gather(keys, 'ctx', axis=0, tiled=True)  30.5 us
    all_gather x1, waiting for transfers between devices, on_device(): lax.all_gather(values, 'ctx', axis=0, tiled=True)  27.2 us
    gather x1, local copies, waits for them, and re-layouts, on_device(): every_key[key_index].reshape(block_count, LIST * BLK, kv_heads, HD)  20.4 us
    gather x1, local copies, waits for them, and re-layouts, on_device(): every_value[key_index].reshape(block_count, LIST * BLK, kv_heads, HD)  20.4 us
    sub x1, other arithmetic, attend_listed(): weights = jnp.where(allowed, jnp.exp(masked - row_max), 0.0)  19.6 us
    dot_general x1, matrix products, attend_listed(): jnp.einsum('bqkgd,blkd->bkgql', block_query, chosen_keys, preferred_eleme...  10.5 us
  transfers between devices with their start and end apart: 4, of which 4 were waited for; matrix products, arithmetic and copies ran while one was open for 17% of the time, Pallas kernels for 0%

commit v1 on v0

--- a/solution.py
+++ b/solution.py
@@ -89,7 +89,9 @@
 
 
 def on_device(x_tokens, w_query, w_key, w_value, w_output, pattern, doc_lengths):
-    features = lax.all_gather(x_tokens, "tp", axis=1, tiled=True)
+    features = jnp.concatenate(
+        lax.all_to_all(jnp.stack(lax.axis_size("tp") * [x_tokens]), "tp", 0, 0), 1
+    )
     local_rows = features.shape[0]
     query_heads = w_query.shape[1] // HD
     kv_heads = w_key.shape[1] // HD

time: 298 us -> 320 us (1.074)
  local copies, waits for them, and re-layouts: 58.6 us -> 95.5 us
  waiting for transfers between devices: 158 us -> 139 us
  starting transfers between devices: 0.31 us -> 5.16 us
    all_gather x1 -> x0, waiting for transfers between devices: 53.2 us -> none  [on_device(): features = lax.all_gather(x_tokens, 'tp', axis=1, tiled=True)]
    all_to_all x0 -> x1, waiting for transfers between devices: none -> 44 us  [on_device(): lax.all_to_all(jnp.stack(lax.axis_size('tp') * [x_tokens]), 'tp', 0, 0)]
    reshape x0 -> x3, local copies, waits for them, and re-layouts: none -> 17.8 us  [on_device(): jnp.concatenate(lax.all_to_all(jnp.stack(lax.axis_size('tp') * [x_tokens]...]
    dot_general x0 -> x2, local copies, waits for them, and re-layouts: none -> 15.4 us  [the longest x1 11.3 us: on_device(): jnp.dot(features, w_query, preferred_element_type=jnp.float32)]
    all_gather x1, waiting for transfers between devices: 30.5 us -> 18.5 us  [on_device(): lax.all_gather(keys, 'ctx', axis=0, tiled=True)]
    reshape x1 -> x0, matrix products: 8.29 us -> none  [rotate(): split_heads = projected.reshape(projected.shape[0], head_count, HD)]
    dot_general x0 -> x1, matrix products: none -> 8.26 us  [on_device(): jnp.dot(features, w_query, preferred_element_type=jnp.float32)]
    all_to_all x0 -> x1, starting transfers between devices: none -> 4.86 us  [on_device(): lax.all_to_all(jnp.stack(lax.axis_size('tp') * [x_tokens]), 'tp', 0, 0)]
  transfers between devices with their start and end apart: 4 -> 4, of which waited for: 4 -> 4; matrix products, arithmetic and copies ran while one was open for 17% -> 21% of each run, Pallas kernels for 0% -> 0%
where the time goes in v1:
time: 320 us; the launch traced here: 319 us
  waiting for transfers between devices  139 us (43%)
  local copies, waits for them, and re-layouts  95.5 us (30%)
  matrix products  40.6 us (13%)
  other arithmetic  25.2 us (8%)
  between operations  13.3 us (4%)
  starting transfers between devices  5.16 us (2%)
    reduce_scatter x1, waiting for transfers between devices, on_device(): lax.psum_scatter(jnp.dot(attended, w_output, preferred_element_type=jnp.f...  46.1 us
    all_to_all x1, waiting for transfers between devices, on_device(): lax.all_to_all(jnp.stack(lax.axis_size('tp') * [x_tokens]), 'tp', 0, 0)  44 us
    all_gather x1, waiting for transfers between devices, on_device(): lax.all_gather(values, 'ctx', axis=0, tiled=True)  30.6 us
    gather x1, local copies, waits for them, and re-layouts, on_device(): every_key[key_index].reshape(block_count, LIST * BLK, kv_heads, HD)  20.3 us
    gather x1, local copies, waits for them, and re-layouts, on_device(): every_value[key_index].reshape(block_count, LIST * BLK, kv_heads, HD)  20.3 us
    sub x1, other arithmetic, attend_listed(): weights = jnp.where(allowed, jnp.exp(masked - row_max), 0.0)  19.6 us
    all_gather x1, waiting for transfers between devices, on_device(): lax.all_gather(keys, 'ctx', axis=0, tiled=True)  18.5 us
    reshape x3, local copies, waits for them, and re-layouts, on_device(): jnp.concatenate(lax.all_to_all(jnp.stack(lax.axis_size('tp') * [x_tokens]...  17.8 us
  transfers between devices with their start and end apart: 4, of which 4 were waited for; matrix products, arithmetic and copies ran while one was open for 21% of the time, Pallas kernels for 0%

profile of v1, /device:TPU:1, one launch (start us, length us, event | category | flops | bytes accessed | tf_op | source)
XLA Modules:
  0.0 318.9 jit_solution(12147322538177579040)
XLA Ops:
  6.5 3.9 %stack.2 = bf16[4,512,1024]{2,1,0:T(8,128)(2,1)} broadcast(bf16[512,1024]{1,0:T(8,128)(2,1)} %param.7), dimensions={1,2} | broadcast | bytes 5242880 | tf_op jit(solution)/shard_map/stack | solution.py:93
  10.4 4.9 %all-to-all-start = ((bf16[4,512,1024]{2,1,0:T(8,128)(2,1)}), bf16[4,512,1024]{2,1,0:T(8,128)(2,1)}, u32[]{:S(2)}, u32[]{:S(2)}) async-start(bf16[4,512,1024]{2,1,0:T(8,128)(2,1)} %stack.2), calls=%async_computation | async-start | bytes 8388608 | tf_op jit(solution)/shard_map/all_to_all | solution.py:93
  15.3 0.0 all-gather.3.cloned.1.call-start
  15.3 4.1 %copy.52 = bf16[256,4096]{1,0:T(8,128)(2,1)} copy(bf16[256,4096]{0,1:T(8,128)(2,1)} %bitcast.63) | data formatting | bytes 4194304 | tf_op jit(solution)/shard_map/dot_general | solution.py:105
  19.5 0.5 multiply_cosine_fusion
  20.0 44.0 %all-to-all-done = bf16[4,512,1024]{2,1,0:T(8,128)(2,1)} async-done(((bf16[4,512,1024]{2,1,0:T(8,128)(2,1)}), bf16[4,512,1024]{2,1,0:T(8,128)(2,1)}, u32[]{:S(2)}, u32[]{:S(2)}) %all-to-all-start) | async-done | bytes 4194336 | tf_op jit(solution)/shard_map/all_to_all | solution.py:93
  64.0 7.4 %copy.39 = bf16[512,4,1024]{2,1,0:T(4,128)(2,1)} copy(bf16[512,4,1024]{2,0,1:T(8,128)(2,1)} %bitcast.4) | data formatting | bytes 8388608 | tf_op jit(solution)/shard_map/reshape | solution.py:92
  71.4 7.8 %reshape.247 = bf16[512,4096,1]{1,0,2:T(8,128)(2,1)} reshape(bf16[512,4,1024]{2,1,0:T(4,128)(2,1)} %copy.39) | data formatting | bytes 8388608 | tf_op jit(solution)/shard_map/reshape | solution.py:92
  79.2 4.2 %fusion.23 = f32[512,2,128]{0,2,1:T(8,128)S(1)} fusion(bf16[512,4096,1]{1,0,2:T(8,128)(2,1)} %reshape.247, bf16[2,128,4096]{2,1,0:T(8,128)(2,1)} %bitcast.64), kind=kOutput, calls=%fused_computation.51 | convolution fusion | flops 1073741824 | bytes 6815744 | tf_op jit(solution)/shard_map/dot_general | solution.py:105
  83.4 0.1 subtract_convert_fusion
  83.5 0.8 copy.41
  84.3 0.0 all-gather.3.cloned.1.call-update
  84.4 0.0 all-gather.5.cloned.1.call-start
  84.4 2.6 copy.58
  87.1 2.0 convolution_convert_fusion.1
  89.1 0.0 all-gather.5.cloned.1.call-update
  89.1 0.2 reduce-scatter.2.cloned.1.call-start
  89.4 0.1 iota_compare_fusion
  89.4 0.2 and_reduce_fusion
  89.7 0.1 broadcast_bitcast_fusion.1
  89.8 0.1 copy.38
  89.9 0.1 reduce
  90.0 0.1 add.112
  90.1 0.1 broadcast_bitcast_fusion
  90.2 0.1 convert_reduce_fusion
  90.3 11.3 %copy.55 = bf16[1024,4096]{1,0:T(8,128)(2,1)} copy(bf16[1024,4096]{0,1:T(8,128)(2,1)} %bitcast.59) | data formatting | bytes 16777216 | tf_op jit(solution)/shard_map/dot_general | solution.py:102
  101.6 0.1 convert_reduce_fusion.1
  101.7 3.9 %and_and_fusion = pred[4,128,1024]{1,2,0:T(8,128)(4,1)} fusion(s32[4,128]{1,0:T(4,128)S(1)} %bitcast.68, s32[4,1024]{1,0:T(4,128)S(1)} %eq.34, s32[4,128]{1,0:T(4,128)S(1)} %add_add_fusion, s32[4,1024]{1,0:T(4,128)S(1)} %bitcast_add_fusion, pred[4,1024]{1,0:T(4,128)(4,1)S(1)} %bitcast.67), kind=kLoop, calls=%fused_computation.18 | loop fusion | flops 2097152 | bytes 565248 | tf_op jit(solution)/shard_map/and | solution.py:65
  105.6 8.3 %fusion.24 = f32[512,8,128]{0,2,1:T(8,128)S(1)} fusion(bf16[512,4096,1]{1,0,2:T(8,128)(2,1)} %reshape.247, bf16[8,128,4096]{2,1,0:T(8,128)(2,1)} %bitcast.60), kind=kOutput, calls=%fused_computation.52 | convolution fusion | flops 4294967296 | bytes 14680064 | tf_op jit(solution)/shard_map/dot_general | solution.py:102
  113.9 0.3 multiply_subtract_fusion
  114.2 1.3 concatenate.13
  115.5 1.7 copy.43
  117.3 1.3 concatenate.14
  118.6 2.7 copy.44
  121.3 18.5 %all-gather.3.cloned.1.call-done = bf16[16384,256]{1,0:T(8,128)(2,1)} async-done(((bf16[512,256]{1,0:T(8,128)(2,1)}), bf16[16384,256]{1,0:T(8,128)(2,1)}) %all-gather.3.cloned.1.call-update) | async-done | bytes 8388624 | tf_op jit(solution)/shard_map/all_gather | solution.py:110
  139.8 20.3 %gather_fusion = bf16[4096,256]{1,0:T(8,128)(2,1)} fusion(bf16[16384,256]{1,0:T(8,128)(2,1)} %all-gather.3.cloned.1.call-done, s32[4096]{0:T(1024)S(1)} %bitcast_clamp_fusion), kind=kCustom, calls=%fused_computation | custom fusion | bytes 4210688 | tf_op jit(solution)/shard_map/gather | solution.py:117
  160.0 4.0 %reshape.225 = bf16[4,1024,2,128]{3,2,1,0:T(2,128)(2,1)} reshape(bf16[4096,256]{1,0:T(8,128)(2,1)} %gather_fusion) | data formatting | bytes 4194304 | tf_op jit(solution)/shard_map/reshape | solution.py:117
  164.0 30.6 %all-gather.5.cloned.1.call-done = bf16[16384,256]{1,0:T(8,128)(2,1)} async-done(((bf16[512,256]{1,0:T(8,128)(2,1)}), bf16[16384,256]{1,0:T(8,128)(2,1)}) %all-gather.5.cloned.1.call-update) | async-done | bytes 8388624 | tf_op jit(solution)/shard_map/all_gather | solution.py:111
  194.6 20.3 %gather_fusion.1 = bf16[4096,256]{1,0:T(8,128)(2,1)} fusion(bf16[16384,256]{1,0:T(8,128)(2,1)} %all-gather.5.cloned.1.call-done, s32[4096]{0:T(1024)S(1)} %bitcast_clamp_fusion), kind=kCustom, calls=%fused_computation.1 | custom fusion | bytes 4210688 | tf_op jit(solution)/shard_map/gather | solution.py:118
  214.9 4.0 %reshape.226 = bf16[4,1024,2,128]{3,2,1,0:T(2,128)(2,1)} reshape(bf16[4096,256]{1,0:T(8,128)(2,1)} %gather_fusion.1) | data formatting | bytes 4194304 | tf_op jit(solution)/shard_map/reshape | solution.py:118
  218.9 10.5 %fusion.9 = f32[4,2,1024,128,4]{3,2,4,1,0:T(8,128)} fusion(bf16[4,1024,2,128,1]{3,2,1,0,4:T(2,128)(2,1)} %bitcast.61, f32[4,128,2,4,64]{4,1,3,2,0:T(8,128)} %copy.44, f32[4,128,2,4,64]{4,1,3,2,0:T(8,128)S(1)} %copy.43), kind=kOutput, calls=%fused_computation.16 | convolution fusion | flops 1075314688 | bytes 20971520 | tf_op jit(solution)/shard_map/bqkgd,blkd->bkgql/dot_general | solution.py:70
  229.3 19.6 %fusion.22 = (f32[4,2,4,128]{3,2,1,0:T(4,128)S(1)}, bf16[4,2,4,128,1024]{3,4,2,1,0:T(8,128)(2,1)}) fusion(f32[4,2,1024,128,4]{3,2,4,1,0:T(8,128)} %fusion.9, pred[4,128,1024]{1,2,0:T(8,128)(4,1)S(1)} %copy-done.3), kind=kOutput, calls=%fused_computation.50 | output fusion | flops 25166848 | bytes 25706496 | tf_op jit(solution)/shard_map/sub | solution.py:75
  248.9 6.2 %fusion.7 = bf16[4,128,2,4,128]{4,1,3,2,0:T(8,128)(2,1)S(1)} fusion(f32[4,128,2,4]{1,3,2,0:T(4,128)S(1)} %bitcast.70, bf16[4,1024,2,128,1]{3,2,1,0,4:T(2,128)(2,1)S(1)} %bitcast.65, bf16[4,2,4,128,1024]{3,4,2,1,0:T(8,128)(2,1)} %get-tuple-element.14), kind=kOutput, calls=%fused_computation.14 | convolution fusion | flops 1074790400 | bytes 11550720 | tf_op jit(solution)/shard_map/bkgql,blkd->bkgqd/dot_general | solution.py:77
  255.1 0.8 copy.48
  256.0 0.8 convert_element_type.46
  256.7 9.5 %convolution_convert_fusion = bf16[512,4096]{1,0:T(8,128)(2,1)} fusion(bf16[512,1024]{1,0:T(8,128)(2,1)S(1)} %convert_element_type.46, bf16[1024,4096]{1,0:T(8,128)(2,1)} %param.11), kind=kOutput, calls=%fused_computation.10 | convolution fusion | flops 4297064448 | bytes 13631488 | tf_op jit(solution)/shard_map/dot_general | solution.py:131
  266.3 0.0 reduce-scatter.2.cloned.1.call-update
  266.3 46.1 %reduce-scatter.2.cloned.1.call-done = bf16[128,4096]{1,0:T(8,128)(2,1)} async-done(((bf16[512,4096]{1,0:T(8,128)(2,1)}), bf16[128,4096]{1,0:T(8,128)(2,1)}) %reduce-scatter.2.cloned.1.call-update) | async-done | bytes 1048592 | tf_op jit(solution)/shard_map/reduce_scatter | solution.py:130
  (27 shorter events, 0.2 us)
Async XLA Ops:
  6.5 80.5 %copy-start = (bf16[4096,256]{1,0:T(8,128)(2,1)S(1)}, bf16[4096,256]{1,0:T(8,128)(2,1)}, u32[]{:S(2)}) copy-start(bf16[4096,256]{1,0:T(8,128)(2,1)} %param.10) | copy-start | bytes 6291460
  10.4 53.6 %all-to-all-start = ((bf16[4,512,1024]{2,1,0:T(8,128)(2,1)}), bf16[4,512,1024]{2,1,0:T(8,128)(2,1)}, u32[]{:S(2)}, u32[]{:S(2)}) async-start(bf16[4,512,1024]{2,1,0:T(8,128)(2,1)} %stack.2), calls=%async_computation | async-start | bytes 8388608 | tf_op jit(solution)/shard_map/all_to_all | solution.py:93
  15.3 124.5 %all-gather.3.cloned.1.call-start = ((), (), s32[]{:S(2)}) async-start(), calls=%async_computation.2 | async-start | bytes 8650752 | tf_op jit(solution)/shard_map/all_gather | solution.py:110
  84.4 110.2 %all-gather.5.cloned.1.call-start = ((), (), s32[]{:S(2)}) async-start(), calls=%async_computation.3 | async-start | bytes 8650752 | tf_op jit(solution)/shard_map/all_gather | solution.py:111
  87.1 2.4 copy-start.4
  87.1 2.7 copy-start.5
  89.1 223.2 %reduce-scatter.2.cloned.1.call-start = ((), (), s32[]{:S(2)}) async-start(), calls=%async_computation.4 | async-start | bytes 5242880 | tf_op jit(solution)/shard_map/reduce_scatter | solution.py:130
  218.9 10.5 %copy-start.3 = (pred[4,128,1024]{1,2,0:T(8,128)(4,1)S(1)}, pred[4,128,1024]{1,2,0:T(8,128)(4,1)}, u32[]{:S(2)}) copy-start(pred[4,128,1024]{1,2,0:T(8,128)(4,1)} %and_and_fusion) | copy-start | bytes 1572868
  229.3 19.6 %copy-start.2 = (bf16[4,1024,2,128]{3,2,1,0:T(2,128)(2,1)S(1)}, bf16[4,1024,2,128]{3,2,1,0:T(2,128)(2,1)}, u32[]{:S(2)}) copy-start(bf16[4,1024,2,128]{3,2,1,0:T(2,128)(2,1)} %reshape.226) | copy-start | bytes 6291460
  256.7 55.6 %copy-start.1 = (bf16[4096,256]{1,0:T(8,128)(2,1)S(1)}, bf16[4096,256]{1,0:T(8,128)(2,1)}, u32[]{:S(2)}) copy-start(bf16[4096,256]{1,0:T(8,128)(2,1)} %param.10) | copy-start | bytes 6291460
Sparse Core Ops, SparseCore 0:
  84.5 55.2 all-gather.2
  142.0 52.5 all-gather.4
  266.4 45.8 reduce-scatter.1
